TPU v7x, 32 devices: a whole 2x2x4 slice. The times are simulated.
32 devices in a mesh: tm: 8 (over z, y), chan: 4 (over x, core).
Axes of the slice: x: 2, y: 2, z: 4, core: 2. Of those that a mesh axis runs over, the one named last changes fastest.
Arguments:
- record: bfloat16 [1280, 8192], P('chan', 'tm'), may hold values from -200 to 200
- owner: int32 [4], replicated, may hold values from 0 to 7, as said below
- offsets: int32 [4, 16], replicated, may hold values from 0 to 924
Outputs:
- score: float32 [4, 16, 8192], P(None, None, 'tm')
Inputs may be any that keep to these rules, and one draw needn't show every extreme that they name: `owner`: no two batches share a time block, and one batch is always held by the last block. `offsets`: a template lies wholly inside its owner's block.
All inputs are finite; a program needn't handle non-finite values.
Results may differ from a plain program's by a relative error of at most 0.0003.
Values may be sent and summed in bfloat16 or wider, within the bound.
A program may use at most 64 MiB of HBM per device.

v0:
```python
import jax
import jax.numpy as jnp
from jax import lax
from jax.sharding import PartitionSpec as P

L = 100


def from_behind(value, axis, by):
    peers = lax.axis_size(axis)
    pairs = [(i, i + by) for i in range(peers) if 0 <= i + by < peers]
    return lax.ppermute(value, axis, pairs)


def spread(value, axis, root):
    mine = lax.axis_index(axis) == root
    return lax.psum(jnp.where(mine, value, jnp.zeros_like(value)), axis)


def cut_windows(source, starts, taps):
    count = starts.shape[0]
    width = source.shape[0]
    pieces = jax.vmap(lambda s: lax.dynamic_slice_in_dim(source, s, taps, 1))(starts)
    return jnp.swapaxes(pieces, 1, 2).reshape(count, taps * width)


def correlate(weights, extended, taps, samples):
    width = extended.shape[0]
    group = 4

    def group_step(g, acc):
        stack = jnp.concatenate(
            [lax.dynamic_slice_in_dim(extended, g * group + i, samples, 1) for i in range(group)],
            axis=0,
        )
        part_weights = lax.dynamic_slice_in_dim(weights, g * group * width, group * width, 1)
        return acc + jnp.dot(part_weights, stack, preferred_element_type=jnp.float32)

    start_acc = jnp.zeros((weights.shape[0], samples), jnp.float32)
    return lax.fori_loop(0, taps // group, group_step, start_acc)


def on_device(record, owner, offsets):
    width, samples = record.shape
    batches, per_batch = offsets.shape
    taps = L
    rim = from_behind(record[:, : taps - 1], "tm", -1)
    extended = jnp.concatenate([record, rim], axis=1)
    batch_weights = []
    for b in range(batches):
        local_cut = cut_windows(record, offsets[b], taps)
        weights = spread(local_cut, "tm", owner[b])
        batch_weights.append(weights)
    all_weights = jnp.concatenate(batch_weights, axis=0)
    corr_part = correlate(all_weights, extended, taps, samples)
    widened = extended.astype(jnp.float32)
    squares = jnp.sum(widened * widened, axis=0)
    running = jnp.concatenate([jnp.zeros((1,), jnp.float32), jnp.cumsum(squares)])
    energy_part = running[taps : taps + samples] - running[:samples]
    floats = all_weights.astype(jnp.float32)
    tnorm_part = jnp.sum(floats * floats, axis=1)
    corr, energy, tnorm = lax.psum((corr_part, energy_part, tnorm_part), "chan")
    score = corr / jnp.sqrt((energy[None, :] + 1e-05) * tnorm[:, None])
    return score.reshape(batches, per_batch, samples)


def solution(mesh):
    in_specs = (P("chan", "tm"), P(), P())
    out_specs = P(None, None, "tm")
    return jax.shard_map(
        on_device, mesh=mesh, in_specs=in_specs, out_specs=out_specs, check_vma=False
    )
```

profile of v0, /device:TPU:1, one launch (start us, length us, event | category | flops | bytes accessed | tf_op | source)
XLA Modules:
  0.0 402.6 jit_solution(13859064046162637730)
XLA Ops:
  6.5 1.5 fusion.15
  9.1 19.9 %while.20 = (s32[]{:T(128)}, bf16[320,1024]{1,0:T(8,128)(2,1)S(1)}, s32[16,2]{0,1:T(2,128)S(1)}, bf16[16,320,100]{2,1,0:T(8,128)(2,1)S(1)}, s32[]{:T(128)}) while((s32[]{:T(128)}, bf16[320,1024]{1,0:T(8,128)(2,1)S(1)}, s32[16,2]{0,1:T(2,128)S(1)}, bf16[16,320,100]{2,1,0:T(8,128)(2,1)S(1)}, s32[]{:T(128)}) %tuple.115), condition=%wide.while_cond, body=%wide.while_body.sunk | while | flops 2 | bytes 163937 | solution.py:23
  30.6 1.6 select_n.144
  33.1 22.0 %while.21 = (s32[]{:T(128)}, bf16[320,1024]{1,0:T(8,128)(2,1)S(1)}, s32[16,2]{0,1:T(2,128)S(1)}, bf16[16,320,100]{2,1,0:T(8,128)(2,1)S(1)}, s32[]{:T(128)}) while((s32[]{:T(128)}, bf16[320,1024]{1,0:T(8,128)(2,1)S(1)}, s32[16,2]{0,1:T(2,128)S(1)}, bf16[16,320,100]{2,1,0:T(8,128)(2,1)S(1)}, s32[]{:T(128)}) %tuple.116), condition=%wide.while_cond.1, body=%wide.while_body.1.sunk | while | flops 2 | bytes 163937 | solution.py:23
  56.0 1.6 select_n.149
  58.5 22.0 %while.22 = (s32[]{:T(128)}, bf16[320,1024]{1,0:T(8,128)(2,1)S(1)}, s32[16,2]{0,1:T(2,128)S(1)}, bf16[16,320,100]{2,1,0:T(8,128)(2,1)S(1)}, s32[]{:T(128)}) while((s32[]{:T(128)}, bf16[320,1024]{1,0:T(8,128)(2,1)S(1)}, s32[16,2]{0,1:T(2,128)S(1)}, bf16[16,320,100]{2,1,0:T(8,128)(2,1)S(1)}, s32[]{:T(128)}) %tuple.117), condition=%wide.while_cond.2, body=%wide.while_body.2.sunk | while | flops 2 | bytes 163937 | solution.py:23
  81.4 1.6 select_n.154
  84.0 22.0 %while.23 = (s32[]{:T(128)}, bf16[320,1024]{1,0:T(8,128)(2,1)S(1)}, s32[16,2]{0,1:T(2,128)S(1)}, bf16[16,320,100]{2,1,0:T(8,128)(2,1)S(1)}, s32[]{:T(128)}) while((s32[]{:T(128)}, bf16[320,1024]{1,0:T(8,128)(2,1)S(1)}, s32[16,2]{0,1:T(2,128)S(1)}, bf16[16,320,100]{2,1,0:T(8,128)(2,1)S(1)}, s32[]{:T(128)}) %tuple.118), condition=%wide.while_cond.3, body=%wide.while_body.3.sunk | while | flops 2 | bytes 163937 | solution.py:23
  106.9 1.6 select_n.159
  110.0 4.8 %collective-permute-done = bf16[320,99]{1,0:T(8,128)(2,1)S(1)} collective-permute-done((bf16[320,99]{1,0:T(8,128)(2,1)S(1)}, bf16[320,99]{1,0:T(8,128)(2,1)S(1)}, u32[]{:S(2)}, u32[]{:S(2)}) %collective-permute-start) | collective-permute-done | bytes 63392 | tf_op jit(solution)/shard_map/ppermute | solution.py:12
  115.6 150.1 %all-reduce.12.cloned.1.call-done = (bf16[16,32000]{1,0:T(8,128)(2,1)}, bf16[16,32000]{1,0:T(8,128)(2,1)}, bf16[16,32000]{1,0:T(8,128)(2,1)}, bf16[16,32000]{1,0:T(8,128)(2,1)}) async-done(((bf16[16,32000]{1,0:T(8,128)(2,1)}, bf16[16,32000]{1,0:T(8,128)(2,1)}, bf16[16,32000]{1,0:T(8,128)(2,1)}, bf16[16,32000]{1,0:T(8,128)(2,1)}), (bf16[16,32000]{1,0:T(8,128)(2,1)}, bf16[16,32000]{1,0:T(8,128)(2,1)}, ...) | async-done | bytes 4096016 | tf_op jit(solution)/shard_map/psum | solution.py:17
  270.6 93.8 %while.24 = (s32[]{:T(128)}, f32[64,1024]{1,0:T(8,128)}, bf16[64,32000]{1,0:T(8,128)(2,1)}, bf16[320,1123]{1,0:T(8,128)(2,1)S(1)}, s32[]{:T(128)}, /*index=5*/s3...) while((s32[]{:T(128)}, f32[64,1024]{1,0:T(8,128)}, ...), condition=%wide.region_5.6_spmd.clone, body=%wide.region_4.5_spmd.clone.sunk | while | flops 178389008 | bytes 8552849 | solution.py:40
  270.6 1.4 constant_dynamic-slice_fusion.17
  272.1 2.2 fusion.21
  274.3 1.4 constant_dynamic-slice_fusion.17
  275.7 2.3 fusion.21
  278.0 1.4 constant_dynamic-slice_fusion.17
  279.5 2.3 fusion.21
  281.8 1.4 constant_dynamic-slice_fusion.17
  283.2 2.3 fusion.21
  285.5 1.4 constant_dynamic-slice_fusion.17
  287.0 2.3 fusion.21
  289.3 1.4 constant_dynamic-slice_fusion.17
  290.7 2.3 fusion.21
  293.1 1.4 constant_dynamic-slice_fusion.17
  294.5 2.3 fusion.21
  296.8 1.4 constant_dynamic-slice_fusion.17
  298.3 2.3 fusion.21
  300.6 1.4 constant_dynamic-slice_fusion.17
  302.0 2.3 fusion.21
  304.3 1.4 constant_dynamic-slice_fusion.17
  305.8 2.3 fusion.21
  308.1 1.4 constant_dynamic-slice_fusion.17
  309.5 2.3 fusion.21
  311.8 1.4 constant_dynamic-slice_fusion.17
  313.3 2.3 fusion.21
  315.6 1.4 constant_dynamic-slice_fusion.17
  317.0 2.3 fusion.21
  320.8 2.3 fusion.21
  323.1 1.4 constant_dynamic-slice_fusion.17
  324.6 2.3 fusion.21
  326.9 1.4 constant_dynamic-slice_fusion.17
  328.3 2.3 fusion.21
  330.6 1.4 constant_dynamic-slice_fusion.17
  332.1 2.3 fusion.21
  334.4 1.4 constant_dynamic-slice_fusion.17
  335.8 2.3 fusion.21
  338.1 1.4 constant_dynamic-slice_fusion.17
  339.6 2.3 fusion.21
  341.9 1.4 constant_dynamic-slice_fusion.17
  343.3 2.3 fusion.21
  345.7 1.4 constant_dynamic-slice_fusion.17
  347.1 2.3 fusion.21
  349.4 1.4 constant_dynamic-slice_fusion.17
  350.8 2.3 fusion.21
  353.2 1.4 constant_dynamic-slice_fusion.17
  354.6 2.3 fusion.21
  356.9 1.4 constant_dynamic-slice_fusion.17
  358.4 2.3 fusion.21
  360.7 1.4 constant_dynamic-slice_fusion.17
  362.1 2.3 fusion.21
  364.5 5.8 %all-reduce.5 = (f32[64]{0:T(128)S(1)}, f32[1024]{0:T(1024)S(1)}) all-reduce(f32[64]{0:T(128)S(1)} %multiply_reduce_fusion, f32[1024]{0:T(1024)S(1)} %fusion.14), channel_id=1, replica_groups=mesh['tm'=8,'chan'=4] {'chan'}, use_global_device_ids=true, to_apply=%region_12.13 | all-reduce | flops 1088 | bytes 8704 | tf_op jit(solution)/shard_map/psum | solution.py:62
  370.3 23.7 %all-reduce.10.cloned.1.call-done = f32[64,1024]{1,0:T(8,128)} async-done(((f32[64,1024]{1,0:T(8,128)}), f32[64,1024]{1,0:T(8,128)}) %all-reduce.10.cloned.1.call-update) | async-done | bytes 262160 | tf_op jit(solution)/shard_map/psum | solution.py:62
  394.0 1.8 rsqrt_multiply_fusion
  (243 shorter events, 98.9 us)
Async XLA Ops:
  6.5 2.6 copy-start
  6.5 259.2 %all-reduce.12.cloned.1.call-start = ((), (), s32[]{:S(2)}) async-start(), calls=%async_computation.1 | async-start | bytes 8192000 | tf_op jit(solution)/shard_map/psum | solution.py:17
  108.6 285.4 %all-reduce.10.cloned.1.call-start = ((), (), s32[]{:S(2)}) async-start(), calls=%async_computation | async-start | bytes 524288 | tf_op jit(solution)/shard_map/psum | solution.py:62
  108.6 6.1 %collective-permute-start = (bf16[320,99]{1,0:T(8,128)(2,1)S(1)}, bf16[320,99]{1,0:T(8,128)(2,1)S(1)}, u32[]{:S(2)}, u32[]{:S(2)}) collective-permute-start(bf16[320,99]{1,0:T(8,128)(2,1)S(1)} %slice.52), channel_id=1, source_target_pairs={{4,0},{8,4},{12,8},{16,12},{20,16},{24,20},{28,24},{5,1},{9,5},{13... | collective-permute-start | bytes 190088 | tf_op jit(solution)/shard_map/ppermute | solution.py:12
  265.7 1.5 copy-start.4
  267.1 1.3 copy-start.3
  267.3 1.4 copy-start.2
  268.7 1.9 copy-start.1
Sparse Core Ops, SparseCore 0:
  108.7 156.9 all-reduce.11
  364.6 29.3 all-reduce.9
where the time goes:
time: 406 us; the launch traced here: 403 us
  waiting for transfers between devices  179 us (44%)
  local copies, waits for them, and re-layouts  137 us (34%)
  matrix products  58 us (14%)
  between operations  16.2 us (4%)
  blocking collectives  5.81 us (1%)
  other arithmetic  4.49 us (1%)
    psum x1, waiting for transfers between devices, spread(): return lax.psum(jnp.where(mine, value, jnp.zeros_like(value)), axis)  150 us
    gather x192, local copies, waits for them, and re-layouts  84.6 us
    dot_general x25, matrix products, group_step(): jnp.dot(part_weights, stack, preferred_element_type=jnp.float32)  58 us
    dynamic_slice x25, local copies, waits for them, and re-layouts, group_step(): lax.dynamic_slice_in_dim(extended, g * group + i, samples, 1)  35.4 us
    psum x1, waiting for transfers between devices, on_device(): corr, energy, tnorm = lax.psum((corr_part, energy_part, tnorm_part), 'chan')  23.7 us
    select_n x8, local copies, waits for them, and re-layouts, spread(): return lax.psum(jnp.where(mine, value, jnp.zeros_like(value)), axis)  9.88 us
  transfers between devices with their start and end apart: 3, of which 3 were waited for; matrix products, arithmetic and copies ran while one was open for 0% of the time, Pallas kernels for 0%

commit v1 on v0

v1 whole, which is shorter than its diff:
```python
import functools

import jax
import jax.numpy as jnp
from jax import lax
from jax.experimental import pallas as pl
from jax.experimental.pallas import tpu as pltpu
from jax.sharding import PartitionSpec as P

L = 100
FOLD = 8
STEPS = -(-L // FOLD)
RIM = 128
LANES = 256
SUB = 5
MESH = pl.DeviceIdType.MESH
VMEM = pl.BlockSpec(memory_space=pltpu.VMEM)
SMEM = pl.BlockSpec(memory_space=pltpu.SMEM)


def gather_kernel(pairs, batches, owner_ref, x_ref, ext_ref, blocks_ref,
                  own, rim, from_l, from_r, to_r, to_l,
                  pair_sem, rim_sem, rs, rr, ls, lr):
    tm = lax.axis_index("tm")
    p, h = tm // 2, tm % 2
    peer = tm + 1 - 2 * h
    half = own.shape[1]
    width = own.shape[2]
    rows = half // SUB
    chunks = batches * SUB
    has_l, has_r = p > 0, p < pairs - 1

    barrier = pltpu.get_barrier_semaphore()
    pl.semaphore_signal(barrier, inc=1, device_id={"tm": peer}, device_id_type=MESH)

    @pl.when(has_l)
    def _():
        pl.semaphore_signal(barrier, inc=1, device_id={"tm": tm - 2}, device_id_type=MESH)

    @pl.when(has_r)
    def _():
        pl.semaphore_signal(barrier, inc=1, device_id={"tm": tm + 2}, device_id_type=MESH)

    pl.semaphore_wait(barrier, 1 + has_l.astype(jnp.int32) + has_r.astype(jnp.int32))

    swap = pltpu.make_async_remote_copy(
        src_ref=x_ref.at[pl.ds(pl.multiple_of((1 - h) * half, 16), half)],
        dst_ref=own.at[h],
        send_sem=pair_sem.at[0], recv_sem=pair_sem.at[1],
        device_id={"tm": peer}, device_id_type=MESH)
    swap.start()
    keep = pltpu.make_async_copy(
        x_ref.at[pl.ds(pl.multiple_of(h * half, 16), half)], own.at[h], pair_sem.at[2])
    keep.start()
    keep.wait()

    @pl.when(jnp.logical_not(has_l))
    def _():
        from_l[...] = jnp.zeros_like(from_l)

    @pl.when(jnp.logical_not(has_r))
    def _():
        from_r[...] = jnp.zeros_like(from_r)
        rim[...] = jnp.zeros_like(rim)

    swap.wait()

    rim_copy = pltpu.make_async_remote_copy(
        src_ref=own.at[0, :, pl.ds(0, RIM)], dst_ref=rim,
        send_sem=rim_sem.at[0], recv_sem=rim_sem.at[1],
        device_id={"tm": tm - 2}, device_id_type=MESH)

    @pl.when(has_l)
    def _():
        rim_copy.start()

    def right(i):
        return pltpu.make_async_remote_copy(
            src_ref=to_r.at[i], dst_ref=from_l.at[i], send_sem=rs.at[i], recv_sem=rr.at[i],
            device_id={"tm": tm + 2}, device_id_type=MESH)

    def left(i):
        return pltpu.make_async_remote_copy(
            src_ref=to_l.at[i], dst_ref=from_r.at[i], send_sem=ls.at[i], recv_sem=lr.at[i],
            device_id={"tm": tm - 2}, device_id_type=MESH)

    def mine(i):
        who = owner_ref[i // SUB]
        at = pl.ds(pl.multiple_of((i % SUB) * rows, 16), rows)
        return who, jnp.where(who % 2 == 0, own[0, at, :], own[1, at, :])

    def tick(t, carry):
        i = t - p

        @pl.when(jnp.logical_and(i >= 0, i < chunks))
        def _():
            @pl.when(has_l)
            def _():
                right(i).wait_recv()

            @pl.when(has_r)
            def _():
                who, value = mine(i)
                to_r[i] = jnp.where(who // 2 == p, value, from_l[i])
                right(i).start()

        k = t - (pairs - 1 - p)

        @pl.when(jnp.logical_and(k >= 0, k < chunks))
        def _():
            @pl.when(has_r)
            def _():
                left(k).wait_recv()

            @pl.when(has_l)
            def _():
                who, value = mine(k)
                to_l[k] = jnp.where(who // 2 == p, value, from_r[k])
                left(k).start()

        return carry

    lax.fori_loop(0, chunks + pairs - 1, tick, 0)

    def settle(i, carry):
        who, value = mine(i)
        far = jnp.where(who // 2 < p, from_l[i], from_r[i])
        at = pl.ds(pl.multiple_of((i % SUB) * rows, 16), rows)
        blocks_ref[i // SUB, at, :] = jnp.where(who // 2 == p, value, far)
        return carry

    lax.fori_loop(0, chunks, settle, 0)

    @pl.when(has_r)
    def _():
        rim_copy.wait_recv()

    ext_ref[:, :width] = own[0]
    ext_ref[:, width:2 * width] = own[1]
    ext_ref[:, 2 * width:] = rim[...]

    def drain(i, carry):
        @pl.when(has_r)
        def _():
            right(i).wait_send()

        @pl.when(has_l)
        def _():
            left(i).wait_send()

        return carry

    lax.fori_loop(0, chunks, drain, 0)

    @pl.when(has_l)
    def _():
        rim_copy.wait_send()


def gather(owner, record, pairs, batches):
    width, samples = record.shape
    half = width // 2
    chunks = batches * SUB
    slots = pltpu.VMEM((chunks, half // SUB, samples), record.dtype)
    sems = pltpu.SemaphoreType.DMA((chunks,))
    return pl.pallas_call(
        functools.partial(gather_kernel, pairs, batches),
        out_shape=(jax.ShapeDtypeStruct((half, 2 * samples + RIM), record.dtype),
                   jax.ShapeDtypeStruct((batches, half, samples), record.dtype)),
        in_specs=[SMEM, VMEM],
        out_specs=(VMEM, VMEM),
        scratch_shapes=[pltpu.VMEM((2, half, samples), record.dtype),
                        pltpu.VMEM((half, RIM), record.dtype),
                        slots, slots, slots, slots,
                        pltpu.SemaphoreType.DMA((3,)), pltpu.SemaphoreType.DMA((2,)),
                        sems, sems, sems, sems],
        compiler_params=pltpu.CompilerParams(
            collective_id=0, has_side_effects=True, vmem_limit_bytes=40 << 20),
        name="gather_blocks",
    )(owner, record)


def correlate_kernel(per_batch, index_ref, ext_ref, block_ref, corr_ref, energy_ref, tnorm_ref,
                     stack, weights):
    half, span = ext_ref.shape
    samples = block_ref.shape[2]
    reach = corr_ref.shape[2]

    @pl.when(pl.program_id(0) == 0)
    def _():
        wide = ext_ref[...].astype(jnp.float32)
        stack[:half] = ext_ref[...]
        for j in range(1, FOLD):
            stack[j * half:(j + 1) * half] = pltpu.roll(wide, span - j, 1).astype(jnp.bfloat16)
        sums = {1: jnp.broadcast_to(jnp.sum(wide * wide, axis=0, keepdims=True), (8, span))}
        n = 1
        while 2 * n <= L:
            sums[2 * n] = sums[n] + pltpu.roll(sums[n], span - n, 1)
            n *= 2
        done, total = 0, None
        for n in sorted(sums, reverse=True):
            if n & L:
                term = sums[n] if done == 0 else pltpu.roll(sums[n], span - done, 1)
                total = term if total is None else total + term
                done += n
        energy_ref[...] = total[:, :reach]

    block = block_ref[0]
    row = lax.broadcasted_iota(jnp.int32, (samples, LANES), 0)
    norm = jnp.zeros((1, LANES), jnp.float32)
    for j in range(FOLD):
        hot = jnp.where(row == index_ref[0, j:j + 1, :], 1.0, 0.0).astype(jnp.bfloat16)
        part = jnp.dot(block, hot, preferred_element_type=jnp.float32)
        norm = norm + jnp.sum(part * part, axis=0, keepdims=True)
        weights[j * half:(j + 1) * half] = part.astype(jnp.bfloat16)
    tnorm_ref[0] = norm
    used = STEPS * per_batch
    turned = weights[...].T[:used]
    grid = jnp.dot(turned, stack[...], preferred_element_type=jnp.float32)
    acc = grid[:per_batch]
    for s in range(1, STEPS):
        acc = acc + pltpu.roll(grid[s * per_batch:(s + 1) * per_batch], span - s * FOLD, 1)
    corr_ref[0] = acc[:, :reach]


def correlate(index, ext, blocks, per_batch):
    batches, half, samples = blocks.shape
    span = ext.shape[1]
    reach = span - RIM
    return pl.pallas_call(
        functools.partial(correlate_kernel, per_batch),
        grid=(batches,),
        out_shape=(jax.ShapeDtypeStruct((batches, per_batch, reach), jnp.float32),
                   jax.ShapeDtypeStruct((8, reach), jnp.float32),
                   jax.ShapeDtypeStruct((batches, 1, LANES), jnp.float32)),
        in_specs=[pl.BlockSpec((1, FOLD, LANES), lambda b: (b, 0, 0)),
                  pl.BlockSpec((half, span), lambda b: (0, 0)),
                  pl.BlockSpec((1, half, samples), lambda b: (b, 0, 0))],
        out_specs=(pl.BlockSpec((1, per_batch, reach), lambda b: (b, 0, 0)),
                   pl.BlockSpec((8, reach), lambda b: (0, 0)),
                   pl.BlockSpec((1, 1, LANES), lambda b: (b, 0, 0))),
        scratch_shapes=[pltpu.VMEM((FOLD * half, span), jnp.bfloat16),
                        pltpu.VMEM((FOLD * half, LANES), jnp.bfloat16)],
        compiler_params=pltpu.CompilerParams(
            dimension_semantics=("arbitrary",), vmem_limit_bytes=48 << 20),
        name="correlate_batches",
    )(index, ext, blocks)


def sum_kernel(peers, part_ref, aux_ref, corr_ref, out_aux_ref,
               got, got_aux, s1, r1, s2, r2, s3, r3):
    tm, c = lax.axis_index("tm"), lax.axis_index("chan")
    h = tm % 2
    samples = corr_ref.shape[2]
    me = h * peers + c
    team = 2 * peers

    def member(i):
        m = lax.rem(me + i, team)
        return m // peers, m % peers

    def target(i):
        hh, cc = member(i)
        return {"tm": tm - h + hh, "chan": cc}

    barrier = pltpu.get_barrier_semaphore()
    for i in range(1, team):
        pl.semaphore_signal(barrier, inc=1, device_id=target(i), device_id_type=MESH)
    pl.semaphore_wait(barrier, team - 1)

    def piece(i):
        hh, cc = member(i)
        return pltpu.make_async_remote_copy(
            src_ref=part_ref.at[cc, :, pl.ds(pl.multiple_of(hh * samples, 128), samples)],
            dst_ref=got.at[i], send_sem=s1.at[i], recv_sem=r1.at[i],
            device_id=target(i), device_id_type=MESH)

    def extra(i):
        hh, cc = member(i)
        return pltpu.make_async_remote_copy(
            src_ref=aux_ref.at[hh], dst_ref=got_aux.at[me], send_sem=s2.at[i], recv_sem=r2.at[i],
            device_id=target(i), device_id_type=MESH)

    def extra_from(i):
        whose = lax.rem(me + team - i, team)
        return pltpu.make_async_remote_copy(
            src_ref=aux_ref.at[0], dst_ref=got_aux.at[whose], send_sem=s2.at[i],
            recv_sem=r2.at[i], device_id=target(i), device_id_type=MESH)

    def share(i):
        return pltpu.make_async_remote_copy(
            src_ref=corr_ref.at[c], dst_ref=corr_ref.at[c], send_sem=s3.at[i], recv_sem=r3.at[i],
            device_id={"tm": tm, "chan": lax.rem(c + i, peers)}, device_id_type=MESH)

    def arriving(i):
        whose = lax.rem(c + peers - i, peers)
        return pltpu.make_async_remote_copy(
            src_ref=corr_ref.at[whose], dst_ref=corr_ref.at[whose], send_sem=s3.at[i],
            recv_sem=r3.at[i], device_id={"tm": tm, "chan": whose}, device_id_type=MESH)

    for i in range(1, team):
        piece(i).start()
    for i in range(1, team):
        extra(i).start()
    total = part_ref[c, :, pl.ds(pl.multiple_of(h * samples, 128), samples)]
    for i in range(1, team):
        piece(i).wait_recv()
        total = total + got[i]
    corr_ref[c] = total
    for i in range(1, peers):
        share(i).start()
    got_aux[me] = aux_ref[h]
    for i in range(1, team):
        extra_from(i).wait_recv()
    aux = got_aux[0]
    for i in range(1, team):
        aux = aux + got_aux[i]
    out_aux_ref[...] = aux
    for i in range(1, peers):
        arriving(i).wait_recv()
    for i in range(1, peers):
        share(i).wait_send()
    for i in range(1, team):
        piece(i).wait_send()
        extra(i).wait_send()


def reduce_all(part, aux, peers):
    _, rows, reach = part.shape
    samples = reach // 2
    team = 2 * peers
    many = pltpu.SemaphoreType.DMA((team,))
    few = pltpu.SemaphoreType.DMA((peers,))
    return pl.pallas_call(
        functools.partial(sum_kernel, peers),
        out_shape=(jax.ShapeDtypeStruct((peers, rows, samples), jnp.float32),
                   jax.ShapeDtypeStruct(aux.shape[1:], jnp.float32)),
        in_specs=[VMEM, VMEM],
        out_specs=(VMEM, VMEM),
        scratch_shapes=[pltpu.VMEM((team, rows, samples), jnp.float32),
                        pltpu.VMEM((team,) + aux.shape[1:], jnp.float32),
                        many, many, many, many, few, few],
        compiler_params=pltpu.CompilerParams(
            collective_id=1, has_side_effects=True, vmem_limit_bytes=32 << 20),
        name="sum_channels",
    )(part, aux)


def on_device(pairs, peers, record, owner, offsets):
    samples = record.shape[1]
    batches, per_batch = offsets.shape
    lane = jnp.arange(LANES)
    tap = FOLD * (lane // per_batch)[None, :] + jnp.arange(FOLD)[:, None]
    start = offsets[:, lane % per_batch]
    index = jnp.where(tap[None] < L, start[:, None, :] + tap[None], -1).astype(jnp.int32)

    ext, blocks = gather(owner, record, pairs, batches)
    corr, energy, norms = correlate(index, ext, blocks, per_batch)
    energy = energy[0].reshape(2, samples // 128, 128)
    norms = jnp.broadcast_to(norms.reshape(1, batches * LANES // 128, 128),
                             (2, batches * LANES // 128, 128))
    aux = jnp.concatenate([energy, norms], axis=1)
    part = corr.reshape(peers, batches * per_batch // peers, 2 * samples)
    total, aux = reduce_all(part, aux, peers)
    energy = aux[:samples // 128].reshape(samples)
    norms = aux[samples // 128:].reshape(batches, LANES // per_batch, per_batch).sum(axis=1)
    total = total.reshape(batches, per_batch, samples)
    return total / jnp.sqrt((energy + 1e-05)[None, None, :] * norms[:, :, None])


def solution(mesh):
    run = functools.partial(on_device, mesh.shape["tm"] // 2, mesh.shape["chan"])
    return jax.shard_map(
        run, mesh=mesh, in_specs=(P("chan", "tm"), P(), P()),
        out_specs=P(None, None, "tm"), check_vma=False)
```

time: 406 us -> 112 us (0.28)
  waiting for transfers between devices: 179 us -> 0 us
  local copies, waits for them, and re-layouts: 137 us -> 3.39 us
  Pallas kernels: 0 us -> 107 us
  matrix products: 58 us -> 0 us
  between operations: 16.2 us -> 0.09 us
  blocking collectives: 5.81 us -> 0 us
    psum x2 -> x0, waiting for transfers between devices: 174 us -> none  [the longest x1 150 us: spread(): return lax.psum(jnp.where(mine, value, jnp.zeros_like(value)), axis)]
    pallas_call x0 -> x3, Pallas kernels: none -> 107 us  [the longest x1 65.8 us: gather(): pl.pallas_call(functools.partial(gather_kernel, pairs, batches), out_shap...]
    gather x192 -> x2, local copies, waits for them, and re-layouts: 84.6 us -> 0.8 us  [on_device(): start = offsets[:, lane % per_batch]]
    dot_general x25 -> x0, matrix products: 58 us -> none  [group_step(): jnp.dot(part_weights, stack, preferred_element_type=jnp.float32)]
    dynamic_slice x25 -> x0, local copies, waits for them, and re-layouts: 35.4 us -> none  [group_step(): lax.dynamic_slice_in_dim(extended, g * group + i, samples, 1)]
    select_n x8 -> x0, local copies, waits for them, and re-layouts: 9.88 us -> none  [spread(): return lax.psum(jnp.where(mine, value, jnp.zeros_like(value)), axis)]
    psum x1 -> x0, blocking collectives: 5.81 us -> none  [on_device(): corr, energy, tnorm = lax.psum((corr_part, energy_part, tnorm_part), 'chan')]
    ppermute x1 -> x0, waiting for transfers between devices: 4.78 us -> none  [from_behind(): return lax.ppermute(value, axis, pairs)]
  transfers between devices with their start and end apart: 3 -> 0, of which waited for: 3 -> 0; matrix products, arithmetic and copies ran while one was open for 0% -> 0% of each run, Pallas kernels for 0% -> 0%
where the time goes in v1:
time: 112 us
  Pallas kernels  107 us (96%)
  local copies, waits for them, and re-layouts  3.39 us (3%)
    pallas_call x1, Pallas kernels, gather(): pl.pallas_call(functools.partial(gather_kernel, pairs, batches), out_shap...  65.8 us
    pallas_call x1, Pallas kernels, reduce_all(): pl.pallas_call(functools.partial(sum_kernel, peers), out_shape=(jax.Shape...  30.1 us
    pallas_call x1, Pallas kernels, correlate(): pl.pallas_call(functools.partial(correlate_kernel, per_batch), grid=(batc...  11.4 us
    unnamed x5, local copies, waits for them, and re-layouts  2.51 us

profile of v1, /device:TPU:1, one launch (start us, length us, event | category | flops | bytes accessed | tf_op | source)
XLA Modules:
  0.0 111.6 jit_solution(15727602887514767177)
XLA Ops:
  0.0 0.8 copy.6
  0.8 0.7 gather_fusion
  1.5 0.1 copy.7
  1.6 0.0 copy-start
  1.6 1.1 copy-done
  2.7 0.0 copy-start.1
  2.7 0.7 copy-done.1
  3.4 65.8 %gather_blocks.1 = (bf16[160,2176]{1,0:T(8,128)(2,1)S(1)}, bf16[4,160,1024]{2,1,0:T(8,128)(2,1)S(1)}) custom-call(s32[4]{0:T(128)S(1)} %copy-done.1, bf16[320,1024]{1,0:T(8,128)(2,1)S(1)} %copy-done), custom_call_target="tpu_custom_call" | custom-call | tf_op jit(solution)/shard_map/gather_blocks/pallas_call | solution.py:166
  69.1 11.4 %correlate_batches.1 = (f32[4,16,2048]{2,1,0:T(8,128)S(1)}, f32[8,2048]{1,0:T(8,128)S(1)}, f32[4,1,256]{2,1,0:T(1,128)S(1)}) custom-call(s32[4,8,256]{2,1,0:T(8,128)S(1)} %add_select_fusion.index_ref, bf16[160,2176]{1,0:T(8,128)(2,1)S(1)} %get-tuple-element.12.ext_ref, bf16[4,160,1024]{2,1,0:T(8,128)(2,1)S(1)} %get-tuple-element.13.block_ref), custom_call_target="tpu_custom_call" | custom-call | tf_op jit(solution)/shard_map/correlate_batches/pallas_call | solution.py:230
  80.5 30.1 %sum_channels.1 = (f32[4,16,1024]{2,1,0:T(8,128)S(1)}, f32[16,128]{1,0:T(8,128)S(1)}) custom-call(f32[4,16,2048]{2,1,0:T(8,128)S(1)} %get-tuple-element.14.part_ref, f32[2,16,128]{2,1,0:T(8,128)S(1)} %pad_maximum_fusion.aux_ref), custom_call_target="tpu_custom_call" | custom-call | tf_op jit(solution)/shard_map/sum_channels/pallas_call | solution.py:334
  110.6 0.1 reshape.101
  110.7 0.8 rsqrt_multiply_fusion
  (11 shorter events, 0.1 us)
Async XLA Ops:
  1.6 1.1 copy-start
  2.7 0.7 copy-start.1

commit v2 on v1

--- a/solution.py
+++ b/solution.py
@@ -13,6 +13,7 @@
 RIM = 128
 LANES = 256
 SUB = 5
+SLACK = 3
 MESH = pl.DeviceIdType.MESH
 VMEM = pl.BlockSpec(memory_space=pltpu.VMEM)
 SMEM = pl.BlockSpec(memory_space=pltpu.SMEM)
@@ -20,7 +21,7 @@
 
 def gather_kernel(pairs, batches, owner_ref, x_ref, ext_ref, blocks_ref,
                   own, rim, from_l, from_r, to_r, to_l,
-                  pair_sem, rim_sem, rs, rr, ls, lr):
+                  keep_sem, rim_sem, swap_s, swap_r, rs, rr, ls, lr):
     tm = lax.axis_index("tm")
     p, h = tm // 2, tm % 2
     peer = tm + 1 - 2 * h
@@ -43,14 +44,27 @@
 
     pl.semaphore_wait(barrier, 1 + has_l.astype(jnp.int32) + has_r.astype(jnp.int32))
 
-    swap = pltpu.make_async_remote_copy(
-        src_ref=x_ref.at[pl.ds(pl.multiple_of((1 - h) * half, 16), half)],
-        dst_ref=own.at[h],
-        send_sem=pair_sem.at[0], recv_sem=pair_sem.at[1],
-        device_id={"tm": peer}, device_id_type=MESH)
-    swap.start()
+    def swap(q):
+        return pltpu.make_async_remote_copy(
+            src_ref=x_ref.at[pl.ds(pl.multiple_of((1 - h) * half + q * rows, 16), rows)],
+            dst_ref=own.at[h, pl.ds(pl.multiple_of(q * rows, 16), rows)],
+            send_sem=swap_s.at[q], recv_sem=swap_r.at[q],
+            device_id={"tm": peer}, device_id_type=MESH)
+
+    def swapped(q):
+        return pltpu.make_async_remote_copy(
+            src_ref=x_ref.at[pl.ds(pl.multiple_of((1 - h) * half + q * rows, 16), rows)],
+            dst_ref=own.at[1 - h, pl.ds(pl.multiple_of(q * rows, 16), rows)],
+            send_sem=swap_s.at[q], recv_sem=swap_r.at[q],
+            device_id={"tm": peer}, device_id_type=MESH)
+
+    def send_swap(q, carry):
+        swap(q).start()
+        return carry
+
+    lax.fori_loop(0, SUB, send_swap, 0)
     keep = pltpu.make_async_copy(
-        x_ref.at[pl.ds(pl.multiple_of(h * half, 16), half)], own.at[h], pair_sem.at[2])
+        x_ref.at[pl.ds(pl.multiple_of(h * half, 16), half)], own.at[h], keep_sem)
     keep.start()
     keep.wait()
 
@@ -62,18 +76,12 @@
     def _():
         from_r[...] = jnp.zeros_like(from_r)
         rim[...] = jnp.zeros_like(rim)
-
-    swap.wait()
 
     rim_copy = pltpu.make_async_remote_copy(
         src_ref=own.at[0, :, pl.ds(0, RIM)], dst_ref=rim,
         send_sem=rim_sem.at[0], recv_sem=rim_sem.at[1],
         device_id={"tm": tm - 2}, device_id_type=MESH)
 
-    @pl.when(has_l)
-    def _():
-        rim_copy.start()
-
     def right(i):
         return pltpu.make_async_remote_copy(
             src_ref=to_r.at[i], dst_ref=from_l.at[i], send_sem=rs.at[i], recv_sem=rr.at[i],
@@ -90,7 +98,15 @@
         return who, jnp.where(who % 2 == 0, own[0, at, :], own[1, at, :])
 
     def tick(t, carry):
-        i = t - p
+        @pl.when(t < SUB)
+        def _():
+            swapped(t).wait_recv()
+
+        @pl.when(jnp.logical_and(t == SUB, has_l))
+        def _():
+            rim_copy.start()
+
+        i = t - p * SLACK
 
         @pl.when(jnp.logical_and(i >= 0, i < chunks))
         def _():
@@ -104,7 +120,7 @@
                 to_r[i] = jnp.where(who // 2 == p, value, from_l[i])
                 right(i).start()
 
-        k = t - (pairs - 1 - p)
+        k = t - (pairs - 1 - p) * SLACK
 
         @pl.when(jnp.logical_and(k >= 0, k < chunks))
         def _():
@@ -120,7 +136,7 @@
 
         return carry
 
-    lax.fori_loop(0, chunks + pairs - 1, tick, 0)
+    lax.fori_loop(0, chunks + (pairs - 1) * SLACK, tick, 0)
 
     def settle(i, carry):
         who, value = mine(i)
@@ -151,6 +167,12 @@
         return carry
 
     lax.fori_loop(0, chunks, drain, 0)
+
+    def drain_swap(q, carry):
+        swap(q).wait_send()
+        return carry
+
+    lax.fori_loop(0, SUB, drain_swap, 0)
 
     @pl.when(has_l)
     def _():
@@ -172,7 +194,8 @@
         scratch_shapes=[pltpu.VMEM((2, half, samples), record.dtype),
                         pltpu.VMEM((half, RIM), record.dtype),
                         slots, slots, slots, slots,
-                        pltpu.SemaphoreType.DMA((3,)), pltpu.SemaphoreType.DMA((2,)),
+                        pltpu.SemaphoreType.DMA, pltpu.SemaphoreType.DMA((2,)),
+                        pltpu.SemaphoreType.DMA((SUB,)), pltpu.SemaphoreType.DMA((SUB,)),
                         sems, sems, sems, sems],
         compiler_params=pltpu.CompilerParams(
             collective_id=0, has_side_effects=True, vmem_limit_bytes=40 << 20),

time: 112 us -> 78.2 us (0.70)
  Pallas kernels: 107 us -> 73.6 us
    pallas_call x1, Pallas kernels: 65.8 us -> 45.7 us  [gather(): pl.pallas_call(functools.partial(gather_kernel, pairs, batches), out_shap...]
    pallas_call x1, Pallas kernels: 30.1 us -> 16.5 us  [reduce_all(): pl.pallas_call(functools.partial(sum_kernel, peers), out_shape=(jax.Shape...]
where the time goes in v2:
time: 78.2 us; the launch traced here: 78 us
  Pallas kernels  73.6 us (94%)
  local copies, waits for them, and re-layouts  3.39 us (4%)
  other arithmetic  0.89 us (1%)
    pallas_call x1, Pallas kernels, gather(): pl.pallas_call(functools.partial(gather_kernel, pairs, batches), out_shap...  45.7 us
    pallas_call x1, Pallas kernels, reduce_all(): pl.pallas_call(functools.partial(sum_kernel, peers), out_shape=(jax.Shape...  16.5 us
    pallas_call x1, Pallas kernels, correlate(): pl.pallas_call(functools.partial(correlate_kernel, per_batch), grid=(batc...  11.4 us
    unnamed x5, local copies, waits for them, and re-layouts  2.51 us

profile of v2, /device:TPU:1, one launch (start us, length us, event | category | flops | bytes accessed | tf_op | source)
XLA Modules:
  0.0 78.0 jit_solution(2346682411929433127)
XLA Ops:
  0.0 0.8 copy.6
  0.8 0.7 gather_fusion
  1.5 0.1 copy.7
  1.6 0.0 copy-start
  1.6 1.1 %copy-done = bf16[320,1024]{1,0:T(8,128)(2,1)S(1)} copy-done((bf16[320,1024]{1,0:T(8,128)(2,1)S(1)}, bf16[320,1024]{1,0:T(8,128)(2,1)}, u32[]{:S(2)}) %copy-start) | copy-done | bytes 655384
  2.7 0.0 copy-start.1
  2.7 0.7 copy-done.1
  3.4 45.7 %gather_blocks.1 = (bf16[160,2176]{1,0:T(8,128)(2,1)S(1)}, bf16[4,160,1024]{2,1,0:T(8,128)(2,1)S(1)}) custom-call(s32[4]{0:T(128)S(1)} %copy-done.1, bf16[320,1024]{1,0:T(8,128)(2,1)S(1)} %copy-done), custom_call_target="tpu_custom_call" | custom-call | tf_op jit(solution)/shard_map/gather_blocks/pallas_call | solution.py:188
  49.1 11.4 %correlate_batches.1 = (f32[4,16,2048]{2,1,0:T(8,128)S(1)}, f32[8,2048]{1,0:T(8,128)S(1)}, f32[4,1,256]{2,1,0:T(1,128)S(1)}) custom-call(s32[4,8,256]{2,1,0:T(8,128)S(1)} %add_select_fusion.index_ref, bf16[160,2176]{1,0:T(8,128)(2,1)S(1)} %get-tuple-element.12.ext_ref, bf16[4,160,1024]{2,1,0:T(8,128)(2,1)S(1)} %get-tuple-element.13.block_ref), custom_call_target="tpu_custom_call" | custom-call | tf_op jit(solution)/shard_map/correlate_batches/pallas_call | solution.py:253
  60.5 16.5 %sum_channels.1 = (f32[4,16,1024]{2,1,0:T(8,128)S(1)}, f32[16,128]{1,0:T(8,128)S(1)}) custom-call(f32[4,16,2048]{2,1,0:T(8,128)S(1)} %get-tuple-element.14.part_ref, f32[2,16,128]{2,1,0:T(8,128)S(1)} %pad_maximum_fusion.aux_ref), custom_call_target="tpu_custom_call" | custom-call | tf_op jit(solution)/shard_map/sum_channels/pallas_call | solution.py:357
  77.1 0.1 reshape.101
  77.1 0.8 %rsqrt_multiply_fusion = f32[4,16,1024]{2,1,0:T(8,128)} fusion(f32[4,16,1024]{2,1,0:T(8,128)S(1)} %get-tuple-element.17, f32[4,16]{1,0:T(4,128)S(1)} %reduce_sum.9, f32[1024]{0:T(1024)S(1)} %get-tuple-element.19), kind=kLoop, calls=%fused_computation.1 | loop fusion | flops 131072 | bytes 528640 | tf_op jit(solution)/shard_map/div | solution.py:391
  (11 shorter events, 0.1 us)
Async XLA Ops:
  1.6 1.1 %copy-start = (bf16[320,1024]{1,0:T(8,128)(2,1)S(1)}, bf16[320,1024]{1,0:T(8,128)(2,1)}, u32[]{:S(2)}) copy-start(bf16[320,1024]{1,0:T(8,128)(2,1)} %x_ref.1) | copy-start | bytes 1966084
  2.7 0.7 copy-start.1

commit v3 on v0

v3 whole, which is shorter than its diff:
```python
import functools

import jax
import jax.numpy as jnp
from jax import lax
from jax.experimental import pallas as pl
from jax.experimental.pallas import tpu as pltpu
from jax.sharding import PartitionSpec as P

L = 100
FOLD = 8
STEPS = -(-L // FOLD)
RIM = 128
LANES = 256
SUB = 5
SLACK = 3
MESH = pl.DeviceIdType.MESH
VMEM = pl.BlockSpec(memory_space=pltpu.VMEM)
SMEM = pl.BlockSpec(memory_space=pltpu.SMEM)


def detect_kernel(pairs, peers, per_batch, owner_ref, x_ref, index_ref, corr_ref, out_aux_ref,
                  own, rim, from_l, from_r, to_r, to_l, block, stack, weights, part, aux, got, got_aux,
                  keep_sem, rim_sem, swap_s, swap_r, rs, rr, ls, lr, s1, r1, s2, r2, s3, r3):
    tm, c = lax.axis_index("tm"), lax.axis_index("chan")
    p, h = tm // 2, tm % 2
    peer = tm + 1 - 2 * h
    half, width = own.shape[1:]
    rows = half // SUB
    batches = index_ref.shape[0]
    chunks = batches * SUB
    span = stack.shape[1]
    reach = part.shape[2]
    deep = part.shape[1]
    groups = peers // batches
    team = 2 * peers
    me = h * peers + c
    has_l, has_r = p > 0, p < pairs - 1

    def member(i):
        m = lax.rem(me + i, team)
        return {"tm": tm - h + m // peers, "chan": m % peers}

    barrier = pltpu.get_barrier_semaphore()
    for i in range(1, team):
        pl.semaphore_signal(barrier, inc=1, device_id=member(i), device_id_type=MESH)

    @pl.when(has_l)
    def _():
        pl.semaphore_signal(barrier, inc=1, device_id={"tm": tm - 2}, device_id_type=MESH)

    @pl.when(has_r)
    def _():
        pl.semaphore_signal(barrier, inc=1, device_id={"tm": tm + 2}, device_id_type=MESH)

    pl.semaphore_wait(barrier, team - 1 + has_l.astype(jnp.int32) + has_r.astype(jnp.int32))

    def swap(q):
        return pltpu.make_async_remote_copy(
            src_ref=x_ref.at[pl.ds(pl.multiple_of((1 - h) * half + q * rows, 16), rows)],
            dst_ref=own.at[h, pl.ds(pl.multiple_of(q * rows, 16), rows)],
            send_sem=swap_s.at[q], recv_sem=swap_r.at[q],
            device_id={"tm": peer}, device_id_type=MESH)

    def swapped(q):
        return pltpu.make_async_remote_copy(
            src_ref=x_ref.at[pl.ds(pl.multiple_of((1 - h) * half + q * rows, 16), rows)],
            dst_ref=own.at[1 - h, pl.ds(pl.multiple_of(q * rows, 16), rows)],
            send_sem=swap_s.at[q], recv_sem=swap_r.at[q],
            device_id={"tm": peer}, device_id_type=MESH)

    def send_swap(q, carry):
        swap(q).start()
        return carry

    lax.fori_loop(0, SUB, send_swap, 0)
    keep = pltpu.make_async_copy(
        x_ref.at[pl.ds(pl.multiple_of(h * half, 16), half)], own.at[h], keep_sem)
    keep.start()
    keep.wait()

    @pl.when(jnp.logical_not(has_l))
    def _():
        from_l[...] = jnp.zeros_like(from_l)

    @pl.when(jnp.logical_not(has_r))
    def _():
        from_r[...] = jnp.zeros_like(from_r)
        rim[...] = jnp.zeros_like(rim)

    rim_copy = pltpu.make_async_remote_copy(
        src_ref=own.at[0, :, pl.ds(0, RIM)], dst_ref=rim,
        send_sem=rim_sem.at[0], recv_sem=rim_sem.at[1],
        device_id={"tm": tm - 2}, device_id_type=MESH)

    def right(i):
        return pltpu.make_async_remote_copy(
            src_ref=to_r.at[i], dst_ref=from_l.at[i], send_sem=rs.at[i], recv_sem=rr.at[i],
            device_id={"tm": tm + 2}, device_id_type=MESH)

    def left(i):
        return pltpu.make_async_remote_copy(
            src_ref=to_l.at[i], dst_ref=from_r.at[i], send_sem=ls.at[i], recv_sem=lr.at[i],
            device_id={"tm": tm - 2}, device_id_type=MESH)

    def mine(i):
        who = owner_ref[i // SUB]
        at = pl.ds(pl.multiple_of((i % SUB) * rows, 16), rows)
        return who, jnp.where(who % 2 == 0, own[0, at, :], own[1, at, :])

    def build():
        @pl.when(has_r)
        def _():
            rim_copy.wait_recv()

        stack[:half, :width] = own[0]
        stack[:half, width:2 * width] = own[1]
        stack[:half, 2 * width:] = rim[...]
        wide = stack[:half].astype(jnp.float32)
        for j in range(1, FOLD):
            stack[j * half:(j + 1) * half] = pltpu.roll(wide, span - j, 1).astype(jnp.bfloat16)
        sums = {1: jnp.broadcast_to(jnp.sum(wide * wide, axis=0, keepdims=True), (8, span))}
        n = 1
        while 2 * n <= L:
            sums[2 * n] = sums[n] + pltpu.roll(sums[n], span - n, 1)
            n *= 2
        done, total = 0, None
        for n in sorted(sums, reverse=True):
            if n & L:
                term = sums[n] if done == 0 else pltpu.roll(sums[n], span - done, 1)
                total = term if total is None else total + term
                done += n
        aux[0, :, :width] = total[:1, :width]
        aux[1, :, :width] = total[:1, width:2 * width]

    def piece(chan, hh):
        return pltpu.make_async_remote_copy(
            src_ref=part.at[chan, :, pl.ds(hh * width, width)],
            dst_ref=got.at[me], send_sem=s1.at[chan, hh], recv_sem=r1.at[me],
            device_id={"tm": tm - h + hh, "chan": chan}, device_id_type=MESH)

    def piece_from(i):
        whose = lax.rem(me + team - i, team)
        return pltpu.make_async_remote_copy(
            src_ref=part.at[0, :, pl.ds(0, width)],
            dst_ref=got.at[whose], send_sem=s1.at[0, 0], recv_sem=r1.at[whose],
            device_id=member(i), device_id_type=MESH)

    def other(chan, hh):
        return jnp.logical_or(chan != c, hh != h)

    def compute(b):
        for q in range(SUB):
            i = b * SUB + q
            who, value = mine(i)
            far = jnp.where(who // 2 < p, from_l[i], from_r[i])
            block[q * rows:(q + 1) * rows] = jnp.where(who // 2 == p, value, far)
        row = lax.broadcasted_iota(jnp.int32, (width, LANES), 0)
        index = index_ref[b]
        norm = jnp.zeros((1, LANES), jnp.float32)
        for j in range(FOLD):
            hot = jnp.where(row == index[j:j + 1], 1.0, 0.0).astype(jnp.bfloat16)
            cut = jnp.dot(block[...], hot, preferred_element_type=jnp.float32)
            norm = norm + jnp.sum(cut * cut, axis=0, keepdims=True)
            weights[j * half:(j + 1) * half] = cut.astype(jnp.bfloat16)
        at = pl.ds(pl.multiple_of(width + b * LANES, 128), LANES)
        aux[0, :, at] = norm
        aux[1, :, at] = norm
        turned = weights[...].T[:STEPS * per_batch]
        grid = jnp.dot(turned, stack[...], preferred_element_type=jnp.float32)
        acc = grid[:per_batch]
        for s in range(1, STEPS):
            acc = acc + pltpu.roll(grid[s * per_batch:(s + 1) * per_batch], span - s * FOLD, 1)
        for k in range(groups):
            part[b * groups + k] = acc[k * deep:(k + 1) * deep, :reach]
        for k in range(groups):
            for hh in range(2):
                chan = b * groups + k

                @pl.when(other(chan, hh))
                def _():
                    piece(chan, hh).start()

    def tick(t, carry):
        @pl.when(t < SUB)
        def _():
            swapped(t).wait_recv()

        @pl.when(jnp.logical_and(t == SUB, has_l))
        def _():
            rim_copy.start()

        i = t - p * SLACK

        @pl.when(jnp.logical_and(i >= 0, i < chunks))
        def _():
            @pl.when(has_l)
            def _():
                right(i).wait_recv()

            @pl.when(has_r)
            def _():
                who, value = mine(i)
                to_r[i] = jnp.where(who // 2 == p, value, from_l[i])
                right(i).start()

        k = t - (pairs - 1 - p) * SLACK

        @pl.when(jnp.logical_and(k >= 0, k < chunks))
        def _():
            @pl.when(has_r)
            def _():
                left(k).wait_recv()

            @pl.when(has_l)
            def _():
                who, value = mine(k)
                to_l[k] = jnp.where(who // 2 == p, value, from_r[k])
                left(k).start()

        @pl.when(t == SUB + 2)
        def _():
            build()

        ready = t + 1 - SUB - SLACK * jnp.maximum(p, pairs - 1 - p)

        @pl.when(jnp.logical_and(ready >= 0, lax.rem(ready + chunks * SUB, SUB) == 0))
        def _():
            @pl.when(ready < chunks)
            def _():
                compute(ready // SUB)

        return carry

    lax.fori_loop(0, chunks + (pairs - 1) * SLACK, tick, 0)

    def extra(i):
        return pltpu.make_async_remote_copy(
            src_ref=aux.at[lax.rem(me + i, team) // peers], dst_ref=got_aux.at[me],
            send_sem=s2.at[i], recv_sem=r2.at[i], device_id=member(i), device_id_type=MESH)

    def extra_from(i):
        whose = lax.rem(me + team - i, team)
        return pltpu.make_async_remote_copy(
            src_ref=aux.at[0], dst_ref=got_aux.at[whose], send_sem=s2.at[i],
            recv_sem=r2.at[i], device_id=member(i), device_id_type=MESH)

    def share(i):
        return pltpu.make_async_remote_copy(
            src_ref=corr_ref.at[c], dst_ref=corr_ref.at[c], send_sem=s3.at[i], recv_sem=r3.at[i],
            device_id={"tm": tm, "chan": lax.rem(c + i, peers)}, device_id_type=MESH)

    def arriving(i):
        whose = lax.rem(c + peers - i, peers)
        return pltpu.make_async_remote_copy(
            src_ref=corr_ref.at[whose], dst_ref=corr_ref.at[whose], send_sem=s3.at[i],
            recv_sem=r3.at[i], device_id={"tm": tm, "chan": whose}, device_id_type=MESH)

    for i in range(1, team):
        extra(i).start()
    got[me] = part[c, :, pl.ds(pl.multiple_of(h * width, 128), width)]
    for i in range(1, team):
        piece_from(i).wait_recv()
    total = got[0]
    for i in range(1, team):
        total = total + got[i]
    corr_ref[c] = total
    for i in range(1, peers):
        share(i).start()
    got_aux[me] = aux[h]
    for i in range(1, team):
        extra_from(i).wait_recv()
    both = got_aux[0]
    for i in range(1, team):
        both = both + got_aux[i]
    out_aux_ref[...] = both
    for i in range(1, peers):
        arriving(i).wait_recv()
    for i in range(1, peers):
        share(i).wait_send()
    for i in range(1, team):
        extra(i).wait_send()
    for chan in range(peers):
        for hh in range(2):
            @pl.when(other(chan, hh))
            def _():
                piece(chan, hh).wait_send()

    def drain(i, carry):
        @pl.when(has_r)
        def _():
            right(i).wait_send()

        @pl.when(has_l)
        def _():
            left(i).wait_send()

        return carry

    lax.fori_loop(0, chunks, drain, 0)

    def drain_swap(q, carry):
        swap(q).wait_send()
        return carry

    lax.fori_loop(0, SUB, drain_swap, 0)

    @pl.when(has_l)
    def _():
        rim_copy.wait_send()


def detect(owner, record, index, pairs, peers, per_batch):
    channels, samples = record.shape
    batches = index.shape[0]
    half = channels // 2
    chunks = batches * SUB
    span = 2 * samples + RIM
    deep = batches * per_batch // peers
    team = 2 * peers
    wide = samples + batches * LANES
    slots = pltpu.VMEM((chunks, half // SUB, samples), record.dtype)
    dma = pltpu.SemaphoreType.DMA
    sems = dma((chunks,))
    many, few = dma((team,)), dma((peers,))
    return pl.pallas_call(
        functools.partial(detect_kernel, pairs, peers, per_batch),
        out_shape=(jax.ShapeDtypeStruct((peers, deep, samples), jnp.float32),
                   jax.ShapeDtypeStruct((1, wide), jnp.float32)),
        in_specs=[SMEM, VMEM, VMEM],
        out_specs=(VMEM, VMEM),
        scratch_shapes=[pltpu.VMEM((2, half, samples), record.dtype),
                        pltpu.VMEM((half, RIM), record.dtype),
                        slots, slots, slots, slots,
                        pltpu.VMEM((half, samples), record.dtype),
                        pltpu.VMEM((FOLD * half, span), record.dtype),
                        pltpu.VMEM((FOLD * half, LANES), record.dtype),
                        pltpu.VMEM((peers, deep, 2 * samples), jnp.float32),
                        pltpu.VMEM((2, 1, wide), jnp.float32),
                        pltpu.VMEM((team, deep, samples), jnp.float32),
                        pltpu.VMEM((team, 1, wide), jnp.float32),
                        dma, dma((2,)), dma((SUB,)), dma((SUB,)), sems, sems, sems, sems,
                        dma((peers, 2)), many, many, many, few, few],
        compiler_params=pltpu.CompilerParams(
            collective_id=0, has_side_effects=True, vmem_limit_bytes=50 << 20),
        name="detect",
    )(owner, record, index)


def on_device(pairs, peers, record, owner, offsets):
    samples = record.shape[1]
    batches, per_batch = offsets.shape
    lane = jnp.arange(LANES)
    tap = FOLD * (lane // per_batch)[None, :] + jnp.arange(FOLD)[:, None]
    start = offsets[:, lane % per_batch]
    index = jnp.where(tap[None] < L, start[:, None, :] + tap[None], -1).astype(jnp.int32)

    total, aux = detect(owner, record, index, pairs, peers, per_batch)
    energy = aux[0, :samples]
    norms = aux[0, samples:].reshape(batches, LANES // per_batch, per_batch).sum(axis=1)
    total = total.reshape(batches, per_batch, samples)
    return total / jnp.sqrt((energy + 1e-05)[None, None, :] * norms[:, :, None])


def solution(mesh):
    run = functools.partial(on_device, mesh.shape["tm"] // 2, mesh.shape["chan"])
    return jax.shard_map(
        run, mesh=mesh, in_specs=(P("chan", "tm"), P(), P()),
        out_specs=P(None, None, "tm"), check_vma=False)
```

time: 406 us -> 63.6 us (0.16)
  waiting for transfers between devices: 179 us -> 0 us
  local copies, waits for them, and re-layouts: 137 us -> 3.36 us
  Pallas kernels: 0 us -> 59.1 us
  matrix products: 58 us -> 0 us
  between operations: 16.2 us -> 0.06 us
  blocking collectives: 5.81 us -> 0 us
    psum x2 -> x0, waiting for transfers between devices: 174 us -> none  [the longest x1 150 us: spread(): return lax.psum(jnp.where(mine, value, jnp.zeros_like(value)), axis)]
    gather x192 -> x2, local copies, waits for them, and re-layouts: 84.6 us -> 0.8 us  [on_device(): start = offsets[:, lane % per_batch]]
    pallas_call x0 -> x1, Pallas kernels: none -> 59.1 us  [detect(): pl.pallas_call(functools.partial(detect_kernel, pairs, peers, per_batch),...]
    dot_general x25 -> x0, matrix products: 58 us -> none  [group_step(): jnp.dot(part_weights, stack, preferred_element_type=jnp.float32)]
    dynamic_slice x25 -> x0, local copies, waits for them, and re-layouts: 35.4 us -> none  [group_step(): lax.dynamic_slice_in_dim(extended, g * group + i, samples, 1)]
    select_n x8 -> x0, local copies, waits for them, and re-layouts: 9.88 us -> none  [spread(): return lax.psum(jnp.where(mine, value, jnp.zeros_like(value)), axis)]
    psum x1 -> x0, blocking collectives: 5.81 us -> none  [on_device(): corr, energy, tnorm = lax.psum((corr_part, energy_part, tnorm_part), 'chan')]
    ppermute x1 -> x0, waiting for transfers between devices: 4.78 us -> none  [from_behind(): return lax.ppermute(value, axis, pairs)]
  transfers between devices with their start and end apart: 3 -> 0, of which waited for: 3 -> 0; matrix products, arithmetic and copies ran while one was open for 0% -> 0% of each run, Pallas kernels for 0% -> 0%
where the time goes in v3:
time: 63.6 us; the launch traced here: 63.4 us
  Pallas kernels  59.1 us (93%)
  local copies, waits for them, and re-layouts  3.36 us (5%)
  other arithmetic  0.9 us (1%)
    pallas_call x1, Pallas kernels, detect(): pl.pallas_call(functools.partial(detect_kernel, pairs, peers, per_batch),...  59.1 us
    unnamed x7, local copies, waits for them, and re-layouts  2.49 us

profile of v3, /device:TPU:1, one launch (start us, length us, event | category | flops | bytes accessed | tf_op | source)
XLA Modules:
  0.0 63.4 jit_solution(7864607778150165667)
XLA Ops:
  0.0 0.0 copy-start.2
  0.1 0.7 %copy-done.2 = s32[4,16]{1,0:T(4,128)S(1)} copy-done((s32[4,16]{1,0:T(4,128)S(1)}, s32[4,16]{1,0:T(4,128)}, u32[]{:S(2)}) %copy-start.2) | copy-done | bytes 280
  0.7 0.1 copy.6
  0.8 0.7 %gather_fusion = s32[256,4]{1,0:T(8,128)S(1)} fusion(s32[4,16]{0,1:T(8,128)S(1)} %copy.6, s32[1024]{0:T(1024)S(1)} %pad_clamp_fusion), kind=kCustom, calls=%fused_computation | custom fusion | bytes 9216 | tf_op jit(solution)/shard_map/gather | solution.py:355
  1.5 0.1 copy.7
  1.6 0.0 copy-start.1
  1.6 0.6 %copy-done.1 = s32[4]{0:T(128)S(1)} copy-done((s32[4]{0:T(128)S(1)}, s32[4]{0:T(128)}, u32[]{:S(2)}) %copy-start.1) | copy-done | bytes 40
  2.3 0.0 copy-start
  2.3 1.1 %copy-done = bf16[320,1024]{1,0:T(8,128)(2,1)S(1)} copy-done((bf16[320,1024]{1,0:T(8,128)(2,1)S(1)}, bf16[320,1024]{1,0:T(8,128)(2,1)}, u32[]{:S(2)}) %copy-start) | copy-done | bytes 655384
  3.4 59.1 %detect.1 = (f32[4,16,1024]{2,1,0:T(8,128)S(1)}, f32[1,2048]{1,0:T(1,128)S(1)}) custom-call(s32[4]{0:T(128)S(1)} %copy-done.1, bf16[320,1024]{1,0:T(8,128)(2,1)S(1)} %copy-done, s32[4,8,256]{2,1,0:T(8,128)S(1)} %add_select_fusion.index_ref), custom_call_target="tpu_custom_call" | custom-call | tf_op jit(solution)/shard_map/detect/pallas_call | solution.py:326
  62.5 0.1 reshape_squeeze.3
  62.6 0.8 %rsqrt_multiply_fusion = f32[4,16,1024]{2,1,0:T(8,128)} fusion(f32[4,16,1024]{2,1,0:T(8,128)S(1)} %get-tuple-element.7, f32[4,16]{1,0:T(4,128)S(1)} %reduce_sum.9, f32[1024]{0:T(1024)S(1)} %bitcast.4), kind=kLoop, calls=%fused_computation.1 | loop fusion | flops 131072 | bytes 528640 | tf_op jit(solution)/shard_map/div | solution.py:362
  (8 shorter events, 0.1 us)
Async XLA Ops:
  0.0 0.7 %copy-start.2 = (s32[4,16]{1,0:T(4,128)S(1)}, s32[4,16]{1,0:T(4,128)}, u32[]{:S(2)}) copy-start(s32[4,16]{1,0:T(4,128)} %param.5) | copy-start | bytes 772
  1.6 0.7 %copy-start.1 = (s32[4]{0:T(128)S(1)}, s32[4]{0:T(128)}, u32[]{:S(2)}) copy-start(s32[4]{0:T(128)} %owner_ref.1) | copy-start | bytes 52
  2.3 1.1 %copy-start = (bf16[320,1024]{1,0:T(8,128)(2,1)S(1)}, bf16[320,1024]{1,0:T(8,128)(2,1)}, u32[]{:S(2)}) copy-start(bf16[320,1024]{1,0:T(8,128)(2,1)} %x_ref.1) | copy-start | bytes 1966084

commit v4 on v3

--- a/solution.py
+++ b/solution.py
@@ -181,6 +181,28 @@
                 def _():
                     piece(chan, hh).start()
 
+    def share(i):
+        return pltpu.make_async_remote_copy(
+            src_ref=corr_ref.at[c], dst_ref=corr_ref.at[c], send_sem=s3.at[i], recv_sem=r3.at[i],
+            device_id={"tm": tm, "chan": lax.rem(c + i, peers)}, device_id_type=MESH)
+
+    def arriving(i):
+        whose = lax.rem(c + peers - i, peers)
+        return pltpu.make_async_remote_copy(
+            src_ref=corr_ref.at[whose], dst_ref=corr_ref.at[whose], send_sem=s3.at[i],
+            recv_sem=r3.at[i], device_id={"tm": tm, "chan": whose}, device_id_type=MESH)
+
+    def finish():
+        got[me] = part[c, :, pl.ds(pl.multiple_of(h * width, 128), width)]
+        for i in range(1, team):
+            piece_from(i).wait_recv()
+        total = got[0]
+        for i in range(1, team):
+            total = total + got[i]
+        corr_ref[c] = total
+        for i in range(1, peers):
+            share(i).start()
+
     def tick(t, carry):
         @pl.when(t < SUB)
         def _():
@@ -230,6 +252,10 @@
             def _():
                 compute(ready // SUB)
 
+                @pl.when(ready // SUB == c // groups + 1)
+                def _():
+                    finish()
+
         return carry
 
     lax.fori_loop(0, chunks + (pairs - 1) * SLACK, tick, 0)
@@ -245,28 +271,12 @@
             src_ref=aux.at[0], dst_ref=got_aux.at[whose], send_sem=s2.at[i],
             recv_sem=r2.at[i], device_id=member(i), device_id_type=MESH)
 
-    def share(i):
-        return pltpu.make_async_remote_copy(
-            src_ref=corr_ref.at[c], dst_ref=corr_ref.at[c], send_sem=s3.at[i], recv_sem=r3.at[i],
-            device_id={"tm": tm, "chan": lax.rem(c + i, peers)}, device_id_type=MESH)
-
-    def arriving(i):
-        whose = lax.rem(c + peers - i, peers)
-        return pltpu.make_async_remote_copy(
-            src_ref=corr_ref.at[whose], dst_ref=corr_ref.at[whose], send_sem=s3.at[i],
-            recv_sem=r3.at[i], device_id={"tm": tm, "chan": whose}, device_id_type=MESH)
-
     for i in range(1, team):
         extra(i).start()
-    got[me] = part[c, :, pl.ds(pl.multiple_of(h * width, 128), width)]
-    for i in range(1, team):
-        piece_from(i).wait_recv()
-    total = got[0]
-    for i in range(1, team):
-        total = total + got[i]
-    corr_ref[c] = total
-    for i in range(1, peers):
-        share(i).start()
+    @pl.when(c // groups == batches - 1)
+    def _():
+        finish()
+
     got_aux[me] = aux[h]
     for i in range(1, team):
         extra_from(i).wait_recv()
@@ -327,7 +337,7 @@
         functools.partial(detect_kernel, pairs, peers, per_batch),
         out_shape=(jax.ShapeDtypeStruct((peers, deep, samples), jnp.float32),
                    jax.ShapeDtypeStruct((1, wide), jnp.float32)),
-        in_specs=[SMEM, VMEM, VMEM],
+        in_specs=[SMEM, pl.BlockSpec(memory_space=pl.ANY), VMEM],
         out_specs=(VMEM, VMEM),
         scratch_shapes=[pltpu.VMEM((2, half, samples), record.dtype),
                         pltpu.VMEM((half, RIM), record.dtype),
@@ -352,7 +362,7 @@
     batches, per_batch = offsets.shape
     lane = jnp.arange(LANES)
     tap = FOLD * (lane // per_batch)[None, :] + jnp.arange(FOLD)[:, None]
-    start = offsets[:, lane % per_batch]
+    start = jnp.tile(offsets, (1, LANES // per_batch))
     index = jnp.where(tap[None] < L, start[:, None, :] + tap[None], -1).astype(jnp.int32)
 
     total, aux = detect(owner, record, index, pairs, peers, per_batch)

time: 63.6 us -> 62.8 us (0.987)
  local copies, waits for them, and re-layouts: 3.36 us -> 2.56 us
    gather x2 -> x0, local copies, waits for them, and re-layouts: 0.8 us -> none  [on_device(): start = offsets[:, lane % per_batch]]
    unnamed x7 -> x6, local copies, waits for them, and re-layouts: 2.49 us -> 2.39 us
where the time goes in v4:
time: 62.8 us; the launch traced here: 62.6 us
  Pallas kernels  59.1 us (94%)
  local copies, waits for them, and re-layouts  2.56 us (4%)
  other arithmetic  0.89 us (1%)
    pallas_call x1, Pallas kernels, detect(): pl.pallas_call(functools.partial(detect_kernel, pairs, peers, per_batch),...  59.1 us
    unnamed x6, local copies, waits for them, and re-layouts  2.39 us

profile of v4, /device:TPU:1, one launch (start us, length us, event | category | flops | bytes accessed | tf_op | source)
XLA Modules:
  0.0 62.6 jit_solution(16383200451124823459)
XLA Ops:
  0.0 0.0 copy-start.2
  0.0 0.7 %copy-done.2 = s32[4,16]{1,0:T(4,128)S(1)} copy-done((s32[4,16]{1,0:T(4,128)S(1)}, s32[4,16]{1,0:T(4,128)}, u32[]{:S(2)}) %copy-start.2) | copy-done | bytes 280
  0.7 0.1 tile.9
  0.8 0.0 copy-start.1
  0.8 0.6 %copy-done.1 = s32[4]{0:T(128)S(1)} copy-done((s32[4]{0:T(128)S(1)}, s32[4]{0:T(128)}, u32[]{:S(2)}) %copy-start.1) | copy-done | bytes 40
  1.4 0.0 copy-start
  1.4 1.1 %copy-done = bf16[320,1024]{1,0:T(8,128)(2,1)S(1)} copy-done((bf16[320,1024]{1,0:T(8,128)(2,1)S(1)}, bf16[320,1024]{1,0:T(8,128)(2,1)}, u32[]{:S(2)}) %copy-start) | copy-done | bytes 655384
  2.5 59.1 %detect.1 = (f32[4,16,1024]{2,1,0:T(8,128)S(1)}, f32[1,2048]{1,0:T(1,128)S(1)}) custom-call(s32[4]{0:T(128)S(1)} %copy-done.1, bf16[320,1024]{1,0:T(8,128)(2,1)S(1)} %copy-done, s32[4,8,256]{2,1,0:T(8,128)S(1)} %add_select_fusion.index_ref), custom_call_target="tpu_custom_call" | custom-call | tf_op jit(solution)/shard_map/detect/pallas_call | solution.py:336
  61.7 0.1 reshape_squeeze.3
  61.8 0.8 %rsqrt_multiply_fusion = f32[4,16,1024]{2,1,0:T(8,128)} fusion(f32[4,16,1024]{2,1,0:T(8,128)S(1)} %get-tuple-element.7, f32[4,16]{1,0:T(4,128)S(1)} %reduce_sum.9, f32[1024]{0:T(1024)S(1)} %bitcast.1), kind=kLoop, calls=%fused_computation | loop fusion | flops 131072 | bytes 528640 | tf_op jit(solution)/shard_map/div | solution.py:372
  (7 shorter events, 0.1 us)
Async XLA Ops:
  0.0 0.7 %copy-start.2 = (s32[4,16]{1,0:T(4,128)S(1)}, s32[4,16]{1,0:T(4,128)}, u32[]{:S(2)}) copy-start(s32[4,16]{1,0:T(4,128)} %param.5) | copy-start | bytes 772
  0.8 0.7 %copy-start.1 = (s32[4]{0:T(128)S(1)}, s32[4]{0:T(128)}, u32[]{:S(2)}) copy-start(s32[4]{0:T(128)} %owner_ref.1) | copy-start | bytes 52
  1.4 1.1 %copy-start = (bf16[320,1024]{1,0:T(8,128)(2,1)S(1)}, bf16[320,1024]{1,0:T(8,128)(2,1)}, u32[]{:S(2)}) copy-start(bf16[320,1024]{1,0:T(8,128)(2,1)} %x_ref.1) | copy-start | bytes 1966084

commit v5 on v4

--- a/solution.py
+++ b/solution.py
@@ -337,7 +337,7 @@
         functools.partial(detect_kernel, pairs, peers, per_batch),
         out_shape=(jax.ShapeDtypeStruct((peers, deep, samples), jnp.float32),
                    jax.ShapeDtypeStruct((1, wide), jnp.float32)),
-        in_specs=[SMEM, pl.BlockSpec(memory_space=pl.ANY), VMEM],
+        in_specs=[SMEM, pl.BlockSpec(memory_space=pltpu.HBM), VMEM],
         out_specs=(VMEM, VMEM),
         scratch_shapes=[pltpu.VMEM((2, half, samples), record.dtype),
                         pltpu.VMEM((half, RIM), record.dtype),

time: 62.8 us -> 62.8 us (level)
  no operation moved by 1% of the time
where the time goes in v5:
time: 62.8 us; the launch traced here: 62.6 us
  Pallas kernels  59.1 us (94%)
  local copies, waits for them, and re-layouts  2.56 us (4%)
  other arithmetic  0.89 us (1%)
    pallas_call x1, Pallas kernels, detect(): pl.pallas_call(functools.partial(detect_kernel, pairs, peers, per_batch),...  59.1 us
    unnamed x6, local copies, waits for them, and re-layouts  2.39 us

profile of v5, /device:TPU:1, one launch (start us, length us, event | category | flops | bytes accessed | tf_op | source)
XLA Modules:
  0.0 62.6 jit_solution(16383200451124823459)
XLA Ops:
  0.0 0.0 copy-start.2
  0.0 0.7 %copy-done.2 = s32[4,16]{1,0:T(4,128)S(1)} copy-done((s32[4,16]{1,0:T(4,128)S(1)}, s32[4,16]{1,0:T(4,128)}, u32[]{:S(2)}) %copy-start.2) | copy-done | bytes 280
  0.7 0.1 tile.9
  0.8 0.0 copy-start.1
  0.8 0.6 %copy-done.1 = s32[4]{0:T(128)S(1)} copy-done((s32[4]{0:T(128)S(1)}, s32[4]{0:T(128)}, u32[]{:S(2)}) %copy-start.1) | copy-done | bytes 40
  1.4 0.0 copy-start
  1.4 1.1 %copy-done = bf16[320,1024]{1,0:T(8,128)(2,1)S(1)} copy-done((bf16[320,1024]{1,0:T(8,128)(2,1)S(1)}, bf16[320,1024]{1,0:T(8,128)(2,1)}, u32[]{:S(2)}) %copy-start) | copy-done | bytes 655384
  2.5 59.1 %detect.1 = (f32[4,16,1024]{2,1,0:T(8,128)S(1)}, f32[1,2048]{1,0:T(1,128)S(1)}) custom-call(s32[4]{0:T(128)S(1)} %copy-done.1, bf16[320,1024]{1,0:T(8,128)(2,1)S(1)} %copy-done, s32[4,8,256]{2,1,0:T(8,128)S(1)} %add_select_fusion.index_ref), custom_call_target="tpu_custom_call" | custom-call | tf_op jit(solution)/shard_map/detect/pallas_call | solution.py:336
  61.7 0.1 reshape_squeeze.3
  61.8 0.8 %rsqrt_multiply_fusion = f32[4,16,1024]{2,1,0:T(8,128)} fusion(f32[4,16,1024]{2,1,0:T(8,128)S(1)} %get-tuple-element.7, f32[4,16]{1,0:T(4,128)S(1)} %reduce_sum.9, f32[1024]{0:T(1024)S(1)} %bitcast.1), kind=kLoop, calls=%fused_computation | loop fusion | flops 131072 | bytes 528640 | tf_op jit(solution)/shard_map/div | solution.py:372
  (7 shorter events, 0.1 us)
Async XLA Ops:
  0.0 0.7 %copy-start.2 = (s32[4,16]{1,0:T(4,128)S(1)}, s32[4,16]{1,0:T(4,128)}, u32[]{:S(2)}) copy-start(s32[4,16]{1,0:T(4,128)} %param.5) | copy-start | bytes 772
  0.8 0.7 %copy-start.1 = (s32[4]{0:T(128)S(1)}, s32[4]{0:T(128)}, u32[]{:S(2)}) copy-start(s32[4]{0:T(128)} %owner_ref.1) | copy-start | bytes 52
  1.4 1.1 %copy-start = (bf16[320,1024]{1,0:T(8,128)(2,1)S(1)}, bf16[320,1024]{1,0:T(8,128)(2,1)}, u32[]{:S(2)}) copy-start(bf16[320,1024]{1,0:T(8,128)(2,1)} %x_ref.1) | copy-start | bytes 1966084
